TPU v7x, 32 devices: a whole 2x2x4 slice. The times are simulated.
32 devices in a mesh: shot: 16 (over z, x, core), dom: 2 (over y).
Axes of the slice: x: 2, y: 2, z: 4, core: 2. Of those that a mesh axis runs over, the one named last changes fastest.
Arguments:
- velocity: float32 [16, 128, 256], P('dom', 'shot'), may hold values from 0.15 to 0.4
- epsilon: float32 [16, 128, 256], P('dom', 'shot'), may hold values from 0.05 to 0.3
- forward_state: float32 [16, 4, 16, 128, 256], P('shot', None, 'dom'), may hold values from -1.2 to 1.2
- adjoint_state: float32 [16, 4, 16, 128, 256], P('shot', None, 'dom'), may hold values from -1.2 to 1.2
- source_cell: int32 [16], P('shot'), may hold values from 0 to 524287
- wavelet: float32 [16, 3], P('shot'), may hold values from -6 to 6
- receiver_cells: int32 [16, 256], P('shot'), may hold values from 0 to 524287
- residuals: float32 [16, 4, 256], P('shot'), may hold values from -6 to 6
Outputs:
- velocity_grad: float32 [16, 128, 256], P('dom', 'shot')
- epsilon_grad: float32 [16, 128, 256], P('dom', 'shot')
Inputs may be any that keep to these rules, and one draw needn't show every extreme that they name: `source_cell`: flat grid cell index (z * 128 + x) * 256 + y of each shot's source. `receiver_cells`: flat grid cell indices (z * 128 + x) * 256 + y of each shot's receivers; two receivers may share a cell.
All inputs are finite; a program needn't handle non-finite values.
Results may differ from a plain program's by a relative error of at most 0.00002.
Values sent between devices are 32-bit elements; how exact they have to be, the bound alone decides.
A program may use at most 128 MiB of HBM per device.

v0:
```python
import functools

import jax
import jax.numpy as jnp
from jax import lax
from jax.experimental import pallas as pl
from jax.experimental.pallas import tpu as pltpu
from jax.sharding import PartitionSpec as P

STEPS = 4
PAD = 8
LANES = 128
C1, C2 = 4.0 / 3.0, 1.0 / 12.0
MESH = pl.DeviceIdType.MESH


def kernel(
    shots, doms, chunk,
    vel, eps, fwd, adj, src, wav, rec, res, out_vel, out_eps,
    p0, p1, q0, q1, w0, w1, s0, s1, a0, a1, a2, b0, b1, b2,
    flat0, flat1, dep0, dep1, img1, img2, stiff, stretch, inj, hot,
    gath, term, from_core, from_x, from_z,
    load_sem, own_sem, z_send, x_send, c_send, g_recv,
    halo_send, halo_recv, rc_send, rc_recv, rx_send, rx_recv, rz_send, rz_recv,
):
    depth, width, length = stiff.shape
    rows = vel.shape[1]
    nrec = rec.shape[1]
    zs = shots // 4
    me = lax.axis_index("shot")
    dom = lax.axis_index("dom")
    core = lax.rem(me, 2)
    xi = lax.rem(me // 2, 2)
    zi = me // 4
    n_chunks = width // chunk
    n_pairs = depth // 2
    near = 1 if doms == 2 else 2
    groups = ((0, near), (near, n_pairs))

    def shot_at(z, x, c):
        return (z * 2 + x) * 2 + c

    has_low = dom > 0
    has_high = dom < doms - 1

    def first_layer_of(place):
        if doms == 2:
            return 2 * jnp.where(has_low, place, n_pairs - 1 - place)
        end = jnp.where(place == 1, n_pairs - 1, place - 1)
        return 2 * jnp.where(place == 0, 0, end)

    loads = []

    def load(source, target):
        copy = pltpu.make_async_copy(source, target, load_sem.at[len(loads)])
        copy.start()
        loads.append(copy)

    own = []
    for place in range(n_pairs):
        pair = pl.ds(first_layer_of(place), 2)
        for i, model in enumerate((vel, eps)):
            copy = pltpu.make_async_copy(
                model.at[pair], gath.at[me, place, i], own_sem.at[place, i])
            copy.start()
            own.append(copy)
    inner = pl.ds(PAD, width)
    cells = pl.ds(2, depth)
    load(adj.at[0, 1], a1)
    load(adj.at[0, 3], b1)
    tiles = length // LANES
    for t in range(tiles):
        load(fwd.at[0, 1, :, :, pl.ds(t * LANES, LANES)], p1.at[:, t, inner, :])
    load(fwd.at[0, 3], q1.at[cells])
    for t in range(tiles):
        load(fwd.at[0, 0, :, :, pl.ds(t * LANES, LANES)], p0.at[:, t, inner, :])
    load(fwd.at[0, 2], q0.at[cells])
    load(adj.at[0, 0], a0)
    load(adj.at[0, 2], b0)

    barrier = pltpu.get_barrier_semaphore()
    for d in range(1, zs):
        pl.semaphore_signal(
            barrier, inc=1, device_id={"shot": shot_at(lax.rem(zi + d, zs), xi, core)},
            device_id_type=MESH)
    pl.semaphore_signal(
        barrier, inc=1, device_id={"shot": shot_at(zi, 1 - xi, core)}, device_id_type=MESH)
    pl.semaphore_signal(
        barrier, inc=1, device_id={"shot": shot_at(zi, xi, 1 - core)}, device_id_type=MESH)

    @pl.when(has_low)
    def _():
        pl.semaphore_signal(barrier, inc=1, device_id={"dom": dom - 1}, device_id_type=MESH)

    @pl.when(has_high)
    def _():
        pl.semaphore_signal(barrier, inc=1, device_id={"dom": dom + 1}, device_id_type=MESH)

    beside = jnp.where(has_low, 1, 0) + jnp.where(has_high, 1, 0)
    pl.semaphore_wait(barrier, zs + 1 + beside)

    def low_copy(source, field, slot):
        return pltpu.make_async_remote_copy(
            src_ref=source, dst_ref=field.at[pl.ds(depth + 2, 2)],
            send_sem=halo_send.at[slot, 0], recv_sem=halo_recv.at[slot, 1],
            device_id={"dom": dom - 1}, device_id_type=MESH)

    def high_copy(source, field, slot):
        return pltpu.make_async_remote_copy(
            src_ref=source, dst_ref=field.at[pl.ds(0, 2)],
            send_sem=halo_send.at[slot, 1], recv_sem=halo_recv.at[slot, 0],
            device_id={"dom": dom + 1}, device_id_type=MESH)

    def send_halo(field, slot, low=None, high=None):
        low = field.at[pl.ds(2, 2)] if low is None else low
        high = field.at[pl.ds(depth, 2)] if high is None else high

        @pl.when(has_low)
        def _():
            low_copy(low, field, slot).start()

        @pl.when(has_high)
        def _():
            high_copy(high, field, slot).start()

    def wait_halo(field, slot):
        @pl.when(has_low)
        def _():
            low_copy(field.at[pl.ds(2, 2)], field, slot).wait_send()
            high_copy(field.at[pl.ds(depth, 2)], field, slot).wait_recv()

        @pl.when(has_high)
        def _():
            high_copy(field.at[pl.ds(depth, 2)], field, slot).wait_send()
            low_copy(field.at[pl.ds(2, 2)], field, slot).wait_recv()

    send_halo(q1, 0, fwd.at[0, 3, pl.ds(0, 2)], fwd.at[0, 3, pl.ds(depth - 2, 2)])

    def block_copy(g, owner, target, send_sem):
        low, high = groups[g]
        part = gath.at[owner, pl.ds(low, high - low)]
        return pltpu.make_async_remote_copy(
            src_ref=part, dst_ref=part, send_sem=send_sem, recv_sem=g_recv.at[g, owner],
            device_id={"shot": target}, device_id_type=MESH)

    def to_x(g, z):
        return block_copy(
            g, shot_at(z, xi, core), shot_at(zi, 1 - xi, core), x_send.at[g, z])

    def to_core(g, z, x):
        return block_copy(
            g, shot_at(z, x, core), shot_at(zi, xi, 1 - core), c_send.at[g, z * 2 + x])

    def to_z(g, d):
        return block_copy(
            g, me, shot_at(lax.rem(zi + d, zs), xi, core), z_send.at[g, d])

    def arrived(g, owner):
        block_copy(g, owner, me, x_send.at[g, 0]).wait_recv()

    def from_z_side(g, d):
        other = lax.rem(zi + (zs - d), zs)
        arrived(g, shot_at(other, xi, core))
        to_x(g, other).start()
        to_core(g, other, xi).start()

    def from_x_side(g, d):
        other = lax.rem(zi + (zs - d), zs)
        arrived(g, shot_at(other, 1 - xi, core))
        to_core(g, other, 1 - xi).start()

    def finish_gather(g):
        for z in range(zs):
            for x in range(2):
                arrived(g, shot_at(z, x, 1 - core))
        for d in range(1, zs):
            to_z(g, d).wait_send()
        for z in range(zs):
            to_x(g, z).wait_send()
            for x in range(2):
                to_core(g, z, x).wait_send()

        def spread(place, carry):
            pair = pl.ds(first_layer_of(place), 2)
            for s in range(shots):
                part = slice(s * rows, (s + 1) * rows)
                speed = gath[s, place, 0]
                stiff[pair, part, :] = speed * speed
                stretch[pair, part, :] = 1.0 + 2.0 * gath[s, place, 1]
            return carry

        lax.fori_loop(*groups[g], spread, 0)

    for copy in own:
        copy.wait()
    for g in range(2):
        to_x(g, zi).start()
        for d in range(1, zs):
            to_z(g, d).start()
        to_core(g, zi, xi).start()

    edge = jnp.zeros((depth, tiles, PAD, LANES), jnp.float32)
    for field in (p0, p1, w0, w1):
        field[:, :, 0:PAD, :] = edge
        field[:, :, PAD + width:PAD + width + PAD, :] = edge
    halo = jnp.zeros((2, width, length), jnp.float32)

    @pl.when(dom == 0)
    def _():
        for field in (q0, q1, s0, s1):
            field[0:2] = halo

    @pl.when(dom == doms - 1)
    def _():
        for field in (q0, q1, s0, s1):
            field[depth + 2:depth + 4] = halo

    first_row = dom * (depth * width)
    rec_row = rec[...] // length - first_row
    rec_col = lax.rem(rec[...], length)
    all_rows = depth * width

    def fill_hot(z, carry):
        ids = lax.broadcasted_iota(jnp.int32, (width, nrec), 0) + z * width
        hot[pl.ds(pl.multiple_of(z * width, width), width), :] = jnp.where(
            ids == rec_row, 1.0, 0.0).astype(jnp.bfloat16)
        return carry

    def inject_moment(k):
        col_hit = lax.broadcasted_iota(jnp.int32, (length, nrec), 0) == rec_col
        amount = res[0, k:k + 1, :]
        parts = []
        for _ in range(3):
            part = amount.astype(jnp.bfloat16).astype(jnp.float32)
            parts.append(jnp.where(col_hit, part, 0.0).astype(jnp.bfloat16))
            amount = amount - part

        def fill(z, carry):
            here = hot[pl.ds(pl.multiple_of(z * width, width), width), :]
            total = None
            for part in parts:
                product = lax.dot_general(
                    here, part, (((1,), (1,)), ((), ())),
                    preferred_element_type=jnp.float32)
                total = product if total is None else total + product
            inj[k, z] = total
            return carry

        lax.fori_loop(0, depth, fill, 0)

    lax.fori_loop(0, depth, fill_hot, 0)
    inject_moment(STEPS - 1)
    for d in range(1, zs):
        from_z_side(0, d)
    for d in range(zs):
        from_x_side(0, d)
    for copy in loads:
        copy.wait()
    finish_gather(0)

    lane = lax.broadcasted_iota(jnp.int32, (chunk, LANES), 1)

    def lateral(field, z, r0):
        def at(t, offset):
            return field[z, t, pl.ds(r0 + (PAD + offset), chunk), :]

        centre = [at(t, 0) for t in range(tiles)]

        def shifted(amount):
            turned = [pltpu.roll(t, amount % LANES, 1) for t in centre]
            result = []
            for i in range(tiles):
                if amount > 0:
                    fill = turned[i - 1] if i > 0 else 0.0
                    result.append(jnp.where(lane >= amount, turned[i], fill))
                else:
                    fill = turned[i + 1] if i + 1 < tiles else 0.0
                    result.append(jnp.where(lane < LANES + amount, turned[i], fill))
            return result

        up1, down1, up2, down2 = shifted(1), shifted(-1), shifted(2), shifted(-2)
        result = []
        for t in range(tiles):
            close = (up1[t] + down1[t]) + (at(t, 1) + at(t, -1))
            remote = (up2[t] + down2[t]) + (at(t, 2) + at(t, -2))
            result.append(C1 * close - C2 * remote - 5.0 * centre[t])
        return jnp.concatenate(centre, axis=1), jnp.concatenate(result, axis=1)

    def get_tiles(field, z, r0):
        return jnp.concatenate(
            [field[z, t, pl.ds(r0 + PAD, chunk), :] for t in range(tiles)], axis=1)

    def put_tiles(field, z, r0, value):
        for t in range(tiles):
            field[z, t, pl.ds(r0 + PAD, chunk), :] = value[:, t * LANES:(t + 1) * LANES]

    def vertical(field, z, r0):
        def at(offset):
            return field[z + (2 + offset), pl.ds(r0, chunk), :]

        centre = at(0)
        return centre, C1 * (at(1) + at(-1)) - C2 * (at(2) + at(-2)) - 2.5 * centre

    source_row = src[0] // length - first_row
    source_col = lax.rem(src[0], length)
    row_ids = lax.broadcasted_iota(jnp.int32, (chunk, length), 0)
    col_hit = lax.broadcasted_iota(jnp.int32, (1, length), 1) == source_col
    P_, Q_ = (p0, p1), (q0, q1)
    W_, S_ = (w0, w1), (s0, s1)

    def forward(k, z, r0, place=None, sub=None):
        now, old = (k + 1) % 2, k % 2
        here = (z, pl.ds(r0, chunk), slice(None))
        p_now, flat = lateral(P_[now], z, r0)
        q_now, dep = vertical(Q_[now], z, r0)
        if k + 1 < STEPS:
            st, sr = stiff[here], stretch[here]
            pulse = jnp.where(
                row_ids == source_row - (z * width + r0),
                jnp.where(col_hit, wav[0, k], 0.0), 0.0)
            layer = (z + 2, pl.ds(r0, chunk), slice(None))
            p_old, q_old = get_tiles(P_[old], z, r0), Q_[old][layer]
            p_new = 2.0 * p_now - p_old + st * (sr * flat + dep) + pulse
            q_new = 2.0 * q_now - q_old + st * (flat + dep) + pulse
            put_tiles(P_[old], z, r0, p_new)
            Q_[old][layer] = q_new
        if k == 0:
            flat0[here], dep0[here] = flat, dep
        elif k == 1:
            flat1[here], dep1[here] = flat, dep
        elif k == 2:
            a, b = a1[here], b1[here]
            img1[here] = a * flat
            img2[here] = a * dep + b * (flat + dep)
        else:
            a, b = a0[here], b0[here]
            img1[here] = img1[here] + a * flat
            img2[here] = img2[here] + (a * dep + b * (flat + dep))

    def weigh(slot, z, r0, a, b):
        here = (z, pl.ds(r0, chunk), slice(None))
        st, sr = stiff[here], stretch[here]
        put_tiles(W_[slot], z, r0, st * (sr * a + b))
        S_[slot][z + 2, pl.ds(r0, chunk), :] = st * (a + b)

    def start_adjoint(z, r0, place=None, sub=None):
        here = (z, pl.ds(r0, chunk), slice(None))
        weigh(0, z, r0, a1[here], b1[here])

    def adjoint(k, z, r0, place=None, sub=None):
        turn = STEPS - 1 - k
        old_a, now_a, new_a = ((a0, a1, a0), (a1, a0, a1), (a0, a1, a2), (a1, a2, None))[turn]
        old_b, now_b, new_b = ((b0, b1, b0), (b1, b0, b1), (b0, b1, b2), (b1, b2, None))[turn]
        here = (z, pl.ds(r0, chunk), slice(None))
        a = 2.0 * now_a[here] - old_a[here] + lateral(W_[turn % 2], z, r0)[1] + inj[(k,) + here]
        b = 2.0 * now_b[here] - old_b[here] + vertical(S_[turn % 2], z, r0)[1]
        if new_a is not None:
            new_a[here], new_b[here] = a, b
            weigh((turn + 1) % 2, z, r0, a, b)
        if k == 1:
            flat, dep = flat1[here], dep1[here]
            img1[here] = img1[here] + a * flat
            img2[here] = img2[here] + (a * dep + b * (flat + dep))
        elif k == 0:
            flat, dep = flat0[here], dep0[here]
            one = img1[here] + a * flat
            two = img2[here] + (a * dep + b * (flat + dep))
            st, sr = stiff[here], stretch[here]
            for i in range(chunk // rows):
                part = slice(i * rows, (i + 1) * rows)
                d = r0 // rows + i
                speed = gath[d, place, 0, sub]
                term[d, place, 0, sub] = 2.0 * speed * (sr[part] * one[part] + two[part])
                term[d, place, 1, sub] = 2.0 * st[part] * one[part]

    def sweep(body, g):
        low, high = groups[g]

        def turn(i, carry):
            j = i // n_chunks
            place, sub = low + j // 2, lax.rem(j, 2)
            r0 = pl.multiple_of(lax.rem(i, n_chunks) * chunk, chunk)
            body(first_layer_of(place) + sub, r0, place, sub)
            return carry

        lax.fori_loop(0, (high - low) * 2 * n_chunks, turn, 0)

    sweep(start_adjoint, 0)
    send_halo(s0, 4)
    if zs > 1:
        from_z_side(1, 1)
    wait_halo(q1, 0)
    sweep(functools.partial(forward, 0), 0)
    send_halo(q0, 1)
    for d in range(2, zs):
        from_z_side(1, d)
    inject_moment(2)
    inject_moment(1)
    for d in range(zs):
        from_x_side(1, d)
    inject_moment(0)
    finish_gather(1)
    sweep(start_adjoint, 1)
    sweep(functools.partial(forward, 0), 1)
    for turn in range(STEPS - 1):
        k = STEPS - 1 - turn
        wait_halo(S_[turn % 2], 4 + turn)
        sweep(functools.partial(adjoint, k), 0)
        send_halo(S_[(turn + 1) % 2], 5 + turn)
        sweep(functools.partial(adjoint, k), 1)
        f = turn + 1
        if f + 1 < STEPS:
            wait_halo(Q_[(f + 1) % 2], f)
            sweep(functools.partial(forward, f), 0)
            send_halo(Q_[f % 2], f + 1)
            sweep(functools.partial(forward, f), 1)

    def sum_copy(g, owner, target, index, landing, send_sem, recv_sem):
        low, high = groups[g]
        places = pl.ds(low, high - low)
        return pltpu.make_async_remote_copy(
            src_ref=term.at[owner, places], dst_ref=landing.at[index, places],
            send_sem=send_sem.at[g, index], recv_sem=recv_sem.at[g, index],
            device_id={"shot": target}, device_id_type=MESH)

    def core_sum(g, j):
        return sum_copy(
            g, 2 * j + (1 - core), shot_at(zi, xi, 1 - core), j, from_core, rc_send, rc_recv)

    def x_sum(g, z):
        return sum_copy(
            g, shot_at(z, 1 - xi, core), shot_at(zi, 1 - xi, core), z, from_x,
            rx_send, rx_recv)

    def z_sum(g, d):
        owner = shot_at(lax.rem(zi + d, zs), xi, core)
        return sum_copy(g, owner, owner, d, from_z, rz_send, rz_recv)

    pairs = chunk // rows // 2

    def last(g):
        low, high = groups[g]

        def stripe(c, carry):
            r0 = pl.multiple_of(c * chunk, chunk)

            def layer(i, inner_carry):
                place, sub = low + i // 2, lax.rem(i, 2)
                adjoint(0, first_layer_of(place) + sub, r0, place, sub)
                return inner_carry

            lax.fori_loop(0, (high - low) * 2, layer, 0)
            for i in range(pairs):
                core_sum(g, c * pairs + i).start()
            return carry

        lax.fori_loop(0, n_chunks, stripe, 0)

    def add(g, owner, landing, index):
        low, high = groups[g]
        places = pl.ds(low, high - low)
        term[owner, places] = term[owner, places] + landing[index, places]

    order = list(range(1, zs)) + [0]

    def sum_cores(g):
        for x, side in ((1 - xi, True), (xi, False)):
            for d in order:
                z = lax.rem(zi + d, zs)
                j = z * 2 + x
                core_sum(g, j).wait_recv()
                add(g, 2 * j + core, from_core, j)
                if side:
                    x_sum(g, z).start()

    def sum_x(g):
        for d in order:
            z = lax.rem(zi + d, zs)
            x_sum(g, z).wait_recv()
            add(g, shot_at(z, xi, core), from_x, z)
            if d > 0:
                z_sum(g, d).start()

    def sum_z(g):
        low, high = groups[g]
        for d in range(1, zs):
            z_sum(g, d).wait_recv()
        for place in range(low, high):
            total = term[me, place]
            for d in range(1, zs):
                total = total + from_z[d, place]
            pair = pl.ds(first_layer_of(place), 2)
            out_vel[pair] = total[0]
            out_eps[pair] = total[1]

    sweep(functools.partial(forward, STEPS - 1), 1)
    last(1)
    sum_cores(1)
    wait_halo(Q_[STEPS % 2], STEPS - 1)
    sweep(functools.partial(forward, STEPS - 1), 0)
    wait_halo(S_[(STEPS - 1) % 2], 3 + STEPS)
    last(0)
    sum_x(1)
    sum_cores(0)
    sum_x(0)
    sum_z(1)
    sum_z(0)
    for g in range(2):
        for j in range(2 * zs):
            core_sum(g, j).wait_send()
        for z in range(zs):
            x_sum(g, z).wait_send()
        for d in range(1, zs):
            z_sum(g, d).wait_send()


def on_device(velocity, epsilon, forward_state, adjoint_state, source_cell, wavelet,
              receiver_cells, residuals, shots, doms):
    depth, width, length = forward_state.shape[2:]
    rows = velocity.shape[1]
    nrec = receiver_cells.shape[1]
    chunk = 64
    zs = shots // 4
    f32 = jnp.float32
    slab = pltpu.VMEM((depth, width, length), f32)
    wide = pltpu.VMEM((depth, length // LANES, width + 2 * PAD, LANES), f32)
    tall = pltpu.VMEM((depth + 4, width, length), f32)
    block = (depth // 2, 2, 2, rows, length)
    dma = pltpu.SemaphoreType.DMA
    scratch = (
        [wide] * 2 + [tall] * 2 + [wide] * 2 + [tall] * 2 + [slab] * 6
        + [slab] * 4 + [slab] * 2 + [slab] * 2
        + [pltpu.VMEM((STEPS, depth, width, length), f32),
           pltpu.VMEM((depth * width, nrec), jnp.bfloat16)]
        + [pltpu.VMEM((shots,) + block, f32), pltpu.VMEM((shots,) + block, f32),
           pltpu.VMEM((2 * zs,) + block, f32), pltpu.VMEM((zs,) + block, f32),
           pltpu.VMEM((zs,) + block, f32)]
        + [dma((6 + 2 * (length // LANES),)), dma((depth // 2, 2)),
           dma((2, zs)), dma((2, zs)), dma((2, 2 * zs)), dma((2, shots)),
           dma((2 * STEPS, 2)), dma((2 * STEPS, 2)),
           dma((2, 2 * zs)), dma((2, 2 * zs)), dma((2, zs)), dma((2, zs)),
           dma((2, zs)), dma((2, zs))]
    )
    vmem = pl.BlockSpec(memory_space=pltpu.VMEM)
    smem = pl.BlockSpec(memory_space=pltpu.SMEM)
    hbm = pl.BlockSpec(memory_space=pl.ANY)
    part = jax.ShapeDtypeStruct((depth, rows, length), f32)
    return pl.pallas_call(
        functools.partial(kernel, shots, doms, chunk),
        out_shape=(part, part),
        in_specs=[hbm, hbm, hbm, hbm, smem, smem, vmem, vmem],
        out_specs=(vmem, vmem),
        scratch_shapes=scratch,
        compiler_params=pltpu.CompilerParams(
            collective_id=0, has_side_effects=True, vmem_limit_bytes=56 * 2**20),
        name="vti_window",
    )(velocity, epsilon, forward_state, adjoint_state, source_cell, wavelet,
      receiver_cells, residuals)


def solution(mesh):
    placed = (
        P("dom", "shot", None),
        P("dom", "shot", None),
        P("shot", None, "dom", None, None),
        P("shot", None, "dom", None, None),
        P("shot"),
        P("shot", None),
        P("shot", None),
        P("shot", None, None),
    )
    return jax.shard_map(
        functools.partial(on_device, shots=mesh.shape["shot"], doms=mesh.shape["dom"]),
        mesh=mesh,
        in_specs=placed,
        out_specs=(P("dom", "shot", None), P("dom", "shot", None)),
        check_vma=False,
    )
```

profile of v0, /device:TPU:0, one launch (start us, length us, event | category | flops | bytes accessed | tf_op | source)
XLA Modules:
  0.0 84.2 jit_solution(16986838913045836341)
XLA Ops:
  1.3 80.0 %vti_window.1 = (f32[8,8,256]{2,1,0:T(8,128)}, f32[8,8,256]{2,1,0:T(8,128)}) custom-call(f32[8,8,256]{2,1,0:T(8,128)} %vel.1, f32[8,8,256]{2,1,0:T(8,128)} %eps.1, f32[1,4,8,128,256]{4,3,2,1,0:T(8,128)} %fwd.1, f32[1,4,8,128,256]{4,3,2,1,0:T(8,128)} %adj.1, s32[1]{0:T(128)S(6)} %copy.12.src, f32[1,3]{1,0:T(1,128)} %wav.1, s32[1,256]{1,0:T(1,128)} %rec.1, ...), custom_call_target="tpu_custom_call" | custom-call | tf_op jit(solution)/shard_map/vti_window/pallas_call | solution.py:548
  81.2 1.5 %copy.13 = f32[8,8,256]{2,1,0:T(8,128)} copy(f32[8,8,256]{2,1,0:T(8,128)} %get-tuple-element.4) | data formatting | bytes 131072
  82.7 1.5 %copy.14 = f32[8,8,256]{2,1,0:T(8,128)} copy(f32[8,8,256]{2,1,0:T(8,128)} %get-tuple-element.5) | data formatting | bytes 131072
where the time goes:
time: 84.4 us; the launch traced here: 84.2 us
  Pallas kernels  80 us (95%)
  local copies, waits for them, and re-layouts  2.95 us (3%)
  between operations  1.29 us (2%)
    pallas_call x1, Pallas kernels, on_device(): pl.pallas_call(functools.partial(kernel, shots, doms, chunk), out_shape=(...  80 us
    unnamed x2, local copies, waits for them, and re-layouts  2.95 us

commit v1 on v0

--- a/solution.py
+++ b/solution.py
@@ -16,7 +16,7 @@
 
 def kernel(
     shots, doms, chunk,
-    vel, eps, fwd, adj, src, wav, rec, res, out_vel, out_eps,
+    vel, eps, fwd, adj, src, wav, rec, res, out,
     p0, p1, q0, q1, w0, w1, s0, s1, a0, a1, a2, b0, b1, b2,
     flat0, flat1, dep0, dep1, img1, img2, stiff, stretch, inj, hot,
     gath, term, from_core, from_x, from_z,
@@ -99,42 +99,48 @@
     beside = jnp.where(has_low, 1, 0) + jnp.where(has_high, 1, 0)
     pl.semaphore_wait(barrier, zs + 1 + beside)
 
-    def low_copy(source, field, slot):
+    def low_copy(source, field, slot, c):
+        stripe = pl.ds(pl.multiple_of(c * chunk, chunk), chunk)
         return pltpu.make_async_remote_copy(
-            src_ref=source, dst_ref=field.at[pl.ds(depth + 2, 2)],
-            send_sem=halo_send.at[slot, 0], recv_sem=halo_recv.at[slot, 1],
+            src_ref=source.at[:, stripe, :], dst_ref=field.at[pl.ds(depth + 2, 2), stripe, :],
+            send_sem=halo_send.at[slot, 0, c], recv_sem=halo_recv.at[slot, 1, c],
             device_id={"dom": dom - 1}, device_id_type=MESH)
 
-    def high_copy(source, field, slot):
+    def high_copy(source, field, slot, c):
+        stripe = pl.ds(pl.multiple_of(c * chunk, chunk), chunk)
         return pltpu.make_async_remote_copy(
-            src_ref=source, dst_ref=field.at[pl.ds(0, 2)],
-            send_sem=halo_send.at[slot, 1], recv_sem=halo_recv.at[slot, 0],
+            src_ref=source.at[:, stripe, :], dst_ref=field.at[pl.ds(0, 2), stripe, :],
+            send_sem=halo_send.at[slot, 1, c], recv_sem=halo_recv.at[slot, 0, c],
             device_id={"dom": dom + 1}, device_id_type=MESH)
 
-    def send_halo(field, slot, low=None, high=None):
+    def send_halo(field, slot, c, low=None, high=None):
         low = field.at[pl.ds(2, 2)] if low is None else low
         high = field.at[pl.ds(depth, 2)] if high is None else high
 
         @pl.when(has_low)
         def _():
-            low_copy(low, field, slot).start()
+            low_copy(low, field, slot, c).start()
 
         @pl.when(has_high)
         def _():
-            high_copy(high, field, slot).start()
-
-    def wait_halo(field, slot):
+            high_copy(high, field, slot, c).start()
+
+    def wait_halo(field, slot, c):
+        low, high = field.at[pl.ds(2, 2)], field.at[pl.ds(depth, 2)]
+
         @pl.when(has_low)
         def _():
-            low_copy(field.at[pl.ds(2, 2)], field, slot).wait_send()
-            high_copy(field.at[pl.ds(depth, 2)], field, slot).wait_recv()
+            low_copy(low, field, slot, c).wait_send()
+            high_copy(high, field, slot, c).wait_recv()
 
         @pl.when(has_high)
         def _():
-            high_copy(field.at[pl.ds(depth, 2)], field, slot).wait_send()
-            low_copy(field.at[pl.ds(2, 2)], field, slot).wait_recv()
-
-    send_halo(q1, 0, fwd.at[0, 3, pl.ds(0, 2)], fwd.at[0, 3, pl.ds(depth - 2, 2)])
+            high_copy(high, field, slot, c).wait_send()
+            low_copy(low, field, slot, c).wait_recv()
+
+    for c in range(n_chunks):
+        send_halo(
+            q1, 0, c, fwd.at[0, 3, pl.ds(0, 2)], fwd.at[0, 3, pl.ds(depth - 2, 2)])
 
     def block_copy(g, owner, target, send_sem):
         low, high = groups[g]
@@ -385,13 +391,27 @@
 
         lax.fori_loop(0, (high - low) * 2 * n_chunks, turn, 0)
 
-    sweep(start_adjoint, 0)
-    send_halo(s0, 4)
+    def near_sweep(body, waits=None, sends=None):
+        def stripe(c, carry):
+            r0 = pl.multiple_of(c * chunk, chunk)
+            if waits is not None:
+                wait_halo(*waits, c)
+
+            def layer(i, inner_carry):
+                body(first_layer_of(i // 2) + lax.rem(i, 2), r0)
+                return inner_carry
+
+            lax.fori_loop(0, near * 2, layer, 0)
+            if sends is not None:
+                send_halo(*sends, c)
+            return carry
+
+        lax.fori_loop(0, n_chunks, stripe, 0)
+
+    near_sweep(start_adjoint, None, (s0, 4))
     if zs > 1:
         from_z_side(1, 1)
-    wait_halo(q1, 0)
-    sweep(functools.partial(forward, 0), 0)
-    send_halo(q0, 1)
+    near_sweep(functools.partial(forward, 0), (q1, 0), (q0, 1))
     for d in range(2, zs):
         from_z_side(1, d)
     inject_moment(2)
@@ -404,15 +424,12 @@
     sweep(functools.partial(forward, 0), 1)
     for turn in range(STEPS - 1):
         k = STEPS - 1 - turn
-        wait_halo(S_[turn % 2], 4 + turn)
-        sweep(functools.partial(adjoint, k), 0)
-        send_halo(S_[(turn + 1) % 2], 5 + turn)
+        near_sweep(functools.partial(adjoint, k), (S_[turn % 2], 4 + turn),
+                   (S_[(turn + 1) % 2], 5 + turn))
         sweep(functools.partial(adjoint, k), 1)
         f = turn + 1
         if f + 1 < STEPS:
-            wait_halo(Q_[(f + 1) % 2], f)
-            sweep(functools.partial(forward, f), 0)
-            send_halo(Q_[f % 2], f + 1)
+            near_sweep(functools.partial(forward, f), (Q_[(f + 1) % 2], f), (Q_[f % 2], f + 1))
             sweep(functools.partial(forward, f), 1)
 
     def sum_copy(g, owner, target, index, landing, send_sem, recv_sem):
@@ -443,6 +460,8 @@
 
         def stripe(c, carry):
             r0 = pl.multiple_of(c * chunk, chunk)
+            if g == 0:
+                wait_halo(S_[(STEPS - 1) % 2], 3 + STEPS, c)
 
             def layer(i, inner_carry):
                 place, sub = low + i // 2, lax.rem(i, 2)
@@ -490,15 +509,13 @@
             for d in range(1, zs):
                 total = total + from_z[d, place]
             pair = pl.ds(first_layer_of(place), 2)
-            out_vel[pair] = total[0]
-            out_eps[pair] = total[1]
+            out[0, pair] = total[0]
+            out[1, pair] = total[1]
 
     sweep(functools.partial(forward, STEPS - 1), 1)
     last(1)
     sum_cores(1)
-    wait_halo(Q_[STEPS % 2], STEPS - 1)
-    sweep(functools.partial(forward, STEPS - 1), 0)
-    wait_halo(S_[(STEPS - 1) % 2], 3 + STEPS)
+    near_sweep(functools.partial(forward, STEPS - 1), (Q_[STEPS % 2], STEPS - 1))
     last(0)
     sum_x(1)
     sum_cores(0)
@@ -537,25 +554,25 @@
            pltpu.VMEM((zs,) + block, f32)]
         + [dma((6 + 2 * (length // LANES),)), dma((depth // 2, 2)),
            dma((2, zs)), dma((2, zs)), dma((2, 2 * zs)), dma((2, shots)),
-           dma((2 * STEPS, 2)), dma((2 * STEPS, 2)),
+           dma((2 * STEPS, 2, width // chunk)), dma((2 * STEPS, 2, width // chunk)),
            dma((2, 2 * zs)), dma((2, 2 * zs)), dma((2, zs)), dma((2, zs)),
            dma((2, zs)), dma((2, zs))]
     )
     vmem = pl.BlockSpec(memory_space=pltpu.VMEM)
     smem = pl.BlockSpec(memory_space=pltpu.SMEM)
     hbm = pl.BlockSpec(memory_space=pl.ANY)
-    part = jax.ShapeDtypeStruct((depth, rows, length), f32)
-    return pl.pallas_call(
+    grads = pl.pallas_call(
         functools.partial(kernel, shots, doms, chunk),
-        out_shape=(part, part),
+        out_shape=jax.ShapeDtypeStruct((2, depth, rows, length), f32),
         in_specs=[hbm, hbm, hbm, hbm, smem, smem, vmem, vmem],
-        out_specs=(vmem, vmem),
+        out_specs=vmem,
         scratch_shapes=scratch,
         compiler_params=pltpu.CompilerParams(
             collective_id=0, has_side_effects=True, vmem_limit_bytes=56 * 2**20),
         name="vti_window",
     )(velocity, epsilon, forward_state, adjoint_state, source_cell, wavelet,
       receiver_cells, residuals)
+    return (grads[0], grads[1])
 
 
 def solution(mesh):

time: 84.4 us -> 82.5 us (0.977)
  local copies, waits for them, and re-layouts: 2.95 us -> 1.53 us
    unnamed x2 -> x0, local copies, waits for them, and re-layouts: 2.95 us -> none
    squeeze x0 -> x1, local copies, waits for them, and re-layouts: none -> 1.53 us  [on_device(): return (grads[0], grads[1])]
where the time goes in v1:
time: 82.5 us; the launch traced here: 82.3 us
  Pallas kernels  79.5 us (96%)
  local copies, waits for them, and re-layouts  1.53 us (2%)
  between operations  1.29 us (2%)
    pallas_call x1, Pallas kernels, on_device(): pl.pallas_call(functools.partial(kernel, shots, doms, chunk), out_shape=j...  79.5 us

profile of v1, /device:TPU:0, one launch (start us, length us, event | category | flops | bytes accessed | tf_op | source)
XLA Modules:
  0.0 82.3 jit_solution(9073906544967955310)
XLA Ops:
  1.3 79.5 %vti_window.1 = f32[2,8,8,256]{3,2,1,0:T(8,128)} custom-call(f32[8,8,256]{2,1,0:T(8,128)} %vel.1, f32[8,8,256]{2,1,0:T(8,128)} %eps.1, f32[1,4,8,128,256]{4,3,2,1,0:T(8,128)} %fwd.1, f32[1,4,8,128,256]{4,3,2,1,0:T(8,128)} %adj.1, s32[1]{0:T(128)S(6)} %copy.10.src, f32[1,3]{1,0:T(1,128)} %wav.1, s32[1,256]{1,0:T(1,128)} %rec.1, f32[1,4,256]{2,1,0:T(4,128)} %res.1), custom_call_target="tpu_custom_call" | custom-call | tf_op jit(solution)/shard_map/vti_window/pallas_call | solution.py:564
  80.8 1.5 %slice_bitcast_fusion = (f32[8,8,256]{2,1,0:T(8,128)}, f32[8,8,256]{2,1,0:T(8,128)}) fusion(f32[2,8,8,256]{3,2,1,0:T(8,128)} %vti_window.1), kind=kLoop, calls=%fused_computation | loop fusion | bytes 262144 | tf_op jit(solution)/shard_map/squeeze | solution.py:575

commit v2 on v1

--- a/solution.py
+++ b/solution.py
@@ -15,7 +15,7 @@
 
 
 def kernel(
-    shots, doms, chunk,
+    shots, doms, chunk, block,
     vel, eps, fwd, adj, src, wav, rec, res, out,
     p0, p1, q0, q1, w0, w1, s0, s1, a0, a1, a2, b0, b1, b2,
     flat0, flat1, dep0, dep1, img1, img2, stiff, stretch, inj, hot,
@@ -232,6 +232,8 @@
             ids == rec_row, 1.0, 0.0).astype(jnp.bfloat16)
         return carry
 
+    span = depth // 2
+
     def inject_moment(k):
         col_hit = lax.broadcasted_iota(jnp.int32, (length, nrec), 0) == rec_col
         amount = res[0, k:k + 1, :]
@@ -241,18 +243,18 @@
             parts.append(jnp.where(col_hit, part, 0.0).astype(jnp.bfloat16))
             amount = amount - part
 
-        def fill(z, carry):
-            here = hot[pl.ds(pl.multiple_of(z * width, width), width), :]
+        def fill(i, carry):
+            here = hot[pl.ds(pl.multiple_of(i * span * width, width), span * width), :]
             total = None
             for part in parts:
                 product = lax.dot_general(
                     here, part, (((1,), (1,)), ((), ())),
                     preferred_element_type=jnp.float32)
                 total = product if total is None else total + product
-            inj[k, z] = total
+            inj[k, pl.ds(i * span, span)] = total.reshape(span, width, length)
             return carry
 
-        lax.fori_loop(0, depth, fill, 0)
+        lax.fori_loop(0, depth // span, fill, 0)
 
     lax.fori_loop(0, depth, fill_hot, 0)
     inject_moment(STEPS - 1)
@@ -264,11 +266,11 @@
         copy.wait()
     finish_gather(0)
 
-    lane = lax.broadcasted_iota(jnp.int32, (chunk, LANES), 1)
+    lane = lax.broadcasted_iota(jnp.int32, (block, LANES), 1)
 
     def lateral(field, z, r0):
         def at(t, offset):
-            return field[z, t, pl.ds(r0 + (PAD + offset), chunk), :]
+            return field[z, t, pl.ds(r0 + (PAD + offset), block), :]
 
         centre = [at(t, 0) for t in range(tiles)]
 
@@ -294,29 +296,29 @@
 
     def get_tiles(field, z, r0):
         return jnp.concatenate(
-            [field[z, t, pl.ds(r0 + PAD, chunk), :] for t in range(tiles)], axis=1)
+            [field[z, t, pl.ds(r0 + PAD, block), :] for t in range(tiles)], axis=1)
 
     def put_tiles(field, z, r0, value):
         for t in range(tiles):
-            field[z, t, pl.ds(r0 + PAD, chunk), :] = value[:, t * LANES:(t + 1) * LANES]
+            field[z, t, pl.ds(r0 + PAD, block), :] = value[:, t * LANES:(t + 1) * LANES]
 
     def vertical(field, z, r0):
         def at(offset):
-            return field[z + (2 + offset), pl.ds(r0, chunk), :]
+            return field[z + (2 + offset), pl.ds(r0, block), :]
 
         centre = at(0)
         return centre, C1 * (at(1) + at(-1)) - C2 * (at(2) + at(-2)) - 2.5 * centre
 
     source_row = src[0] // length - first_row
     source_col = lax.rem(src[0], length)
-    row_ids = lax.broadcasted_iota(jnp.int32, (chunk, length), 0)
+    row_ids = lax.broadcasted_iota(jnp.int32, (block, length), 0)
     col_hit = lax.broadcasted_iota(jnp.int32, (1, length), 1) == source_col
     P_, Q_ = (p0, p1), (q0, q1)
     W_, S_ = (w0, w1), (s0, s1)
 
     def forward(k, z, r0, place=None, sub=None):
         now, old = (k + 1) % 2, k % 2
-        here = (z, pl.ds(r0, chunk), slice(None))
+        here = (z, pl.ds(r0, block), slice(None))
         p_now, flat = lateral(P_[now], z, r0)
         q_now, dep = vertical(Q_[now], z, r0)
         if k + 1 < STEPS:
@@ -324,60 +326,89 @@
             pulse = jnp.where(
                 row_ids == source_row - (z * width + r0),
                 jnp.where(col_hit, wav[0, k], 0.0), 0.0)
-            layer = (z + 2, pl.ds(r0, chunk), slice(None))
+            layer = (z + 2, pl.ds(r0, block), slice(None))
             p_old, q_old = get_tiles(P_[old], z, r0), Q_[old][layer]
             p_new = 2.0 * p_now - p_old + st * (sr * flat + dep) + pulse
             q_new = 2.0 * q_now - q_old + st * (flat + dep) + pulse
-            put_tiles(P_[old], z, r0, p_new)
-            Q_[old][layer] = q_new
-        if k == 0:
-            flat0[here], dep0[here] = flat, dep
-        elif k == 1:
-            flat1[here], dep1[here] = flat, dep
-        elif k == 2:
-            a, b = a1[here], b1[here]
-            img1[here] = a * flat
-            img2[here] = a * dep + b * (flat + dep)
-        else:
-            a, b = a0[here], b0[here]
-            img1[here] = img1[here] + a * flat
-            img2[here] = img2[here] + (a * dep + b * (flat + dep))
+        if k >= 2:
+            a, b = (a1[here], b1[here]) if k == 2 else (a0[here], b0[here])
+            one, two = a * flat, a * dep + b * (flat + dep)
+            if k > 2:
+                one, two = img1[here] + one, img2[here] + two
+
+        def commit():
+            if k + 1 < STEPS:
+                put_tiles(P_[old], z, r0, p_new)
+                Q_[old][layer] = q_new
+            if k == 0:
+                flat0[here], dep0[here] = flat, dep
+            elif k == 1:
+                flat1[here], dep1[here] = flat, dep
+            else:
+                img1[here], img2[here] = one, two
+
+        return commit
 
     def weigh(slot, z, r0, a, b):
-        here = (z, pl.ds(r0, chunk), slice(None))
+        here = (z, pl.ds(r0, block), slice(None))
         st, sr = stiff[here], stretch[here]
-        put_tiles(W_[slot], z, r0, st * (sr * a + b))
-        S_[slot][z + 2, pl.ds(r0, chunk), :] = st * (a + b)
+        weighed, plain = st * (sr * a + b), st * (a + b)
+
+        def commit():
+            put_tiles(W_[slot], z, r0, weighed)
+            S_[slot][z + 2, pl.ds(r0, block), :] = plain
+
+        return commit
 
     def start_adjoint(z, r0, place=None, sub=None):
-        here = (z, pl.ds(r0, chunk), slice(None))
-        weigh(0, z, r0, a1[here], b1[here])
+        here = (z, pl.ds(r0, block), slice(None))
+        return weigh(0, z, r0, a1[here], b1[here])
 
     def adjoint(k, z, r0, place=None, sub=None):
         turn = STEPS - 1 - k
         old_a, now_a, new_a = ((a0, a1, a0), (a1, a0, a1), (a0, a1, a2), (a1, a2, None))[turn]
         old_b, now_b, new_b = ((b0, b1, b0), (b1, b0, b1), (b0, b1, b2), (b1, b2, None))[turn]
-        here = (z, pl.ds(r0, chunk), slice(None))
+        here = (z, pl.ds(r0, block), slice(None))
         a = 2.0 * now_a[here] - old_a[here] + lateral(W_[turn % 2], z, r0)[1] + inj[(k,) + here]
         b = 2.0 * now_b[here] - old_b[here] + vertical(S_[turn % 2], z, r0)[1]
+        commit_weighed = None
         if new_a is not None:
-            new_a[here], new_b[here] = a, b
-            weigh((turn + 1) % 2, z, r0, a, b)
+            commit_weighed = weigh((turn + 1) % 2, z, r0, a, b)
         if k == 1:
             flat, dep = flat1[here], dep1[here]
-            img1[here] = img1[here] + a * flat
-            img2[here] = img2[here] + (a * dep + b * (flat + dep))
+            one = img1[here] + a * flat
+            two = img2[here] + (a * dep + b * (flat + dep))
         elif k == 0:
             flat, dep = flat0[here], dep0[here]
             one = img1[here] + a * flat
             two = img2[here] + (a * dep + b * (flat + dep))
             st, sr = stiff[here], stretch[here]
-            for i in range(chunk // rows):
-                part = slice(i * rows, (i + 1) * rows)
-                d = r0 // rows + i
-                speed = gath[d, place, 0, sub]
-                term[d, place, 0, sub] = 2.0 * speed * (sr[part] * one[part] + two[part])
-                term[d, place, 1, sub] = 2.0 * st[part] * one[part]
+            first = 2.0 * (sr * one + two)
+            second = 2.0 * st * one
+            speeds = [gath[r0 // rows + i, place, 0, sub] for i in range(block // rows)]
+
+        def commit():
+            if new_a is not None:
+                new_a[here], new_b[here] = a, b
+                commit_weighed()
+            if k == 1:
+                img1[here], img2[here] = one, two
+            elif k == 0:
+                for i, speed in enumerate(speeds):
+                    part = slice(i * rows, (i + 1) * rows)
+                    term[r0 // rows + i, place, 0, sub] = speed * first[part]
+                    term[r0 // rows + i, place, 1, sub] = second[part]
+
+        return commit
+
+    def run(body, z, r0, place=None, sub=None):
+        pending = None
+        for i in range(chunk // block):
+            commit = body(z, pl.multiple_of(r0 + i * block, block), place, sub)
+            if pending is not None:
+                pending()
+            pending = commit
+        pending()
 
     def sweep(body, g):
         low, high = groups[g]
@@ -386,7 +417,7 @@
             j = i // n_chunks
             place, sub = low + j // 2, lax.rem(j, 2)
             r0 = pl.multiple_of(lax.rem(i, n_chunks) * chunk, chunk)
-            body(first_layer_of(place) + sub, r0, place, sub)
+            run(body, first_layer_of(place) + sub, r0, place, sub)
             return carry
 
         lax.fori_loop(0, (high - low) * 2 * n_chunks, turn, 0)
@@ -398,7 +429,7 @@
                 wait_halo(*waits, c)
 
             def layer(i, inner_carry):
-                body(first_layer_of(i // 2) + lax.rem(i, 2), r0)
+                run(body, first_layer_of(i // 2) + lax.rem(i, 2), r0)
                 return inner_carry
 
             lax.fori_loop(0, near * 2, layer, 0)
@@ -465,7 +496,7 @@
 
             def layer(i, inner_carry):
                 place, sub = low + i // 2, lax.rem(i, 2)
-                adjoint(0, first_layer_of(place) + sub, r0, place, sub)
+                run(functools.partial(adjoint, 0), first_layer_of(place) + sub, r0, place, sub)
                 return inner_carry
 
             lax.fori_loop(0, (high - low) * 2, layer, 0)
@@ -562,7 +593,7 @@
     smem = pl.BlockSpec(memory_space=pltpu.SMEM)
     hbm = pl.BlockSpec(memory_space=pl.ANY)
     grads = pl.pallas_call(
-        functools.partial(kernel, shots, doms, chunk),
+        functools.partial(kernel, shots, doms, chunk, 16),
         out_shape=jax.ShapeDtypeStruct((2, depth, rows, length), f32),
         in_specs=[hbm, hbm, hbm, hbm, smem, smem, vmem, vmem],
         out_specs=vmem,

time: 82.5 us -> 80.5 us (0.976)
  Pallas kernels: 79.5 us -> 77.5 us
    pallas_call x1, Pallas kernels: 79.5 us -> 77.5 us  [on_device(): pl.pallas_call(functools.partial(kernel, shots, doms, chunk, 16), out_sha...]
where the time goes in v2:
time: 80.5 us; the launch traced here: 80.3 us
  Pallas kernels  77.5 us (96%)
  local copies, waits for them, and re-layouts  1.53 us (2%)
  between operations  1.29 us (2%)
    pallas_call x1, Pallas kernels, on_device(): pl.pallas_call(functools.partial(kernel, shots, doms, chunk, 16), out_sha...  77.5 us

profile of v2, /device:TPU:0, one launch (start us, length us, event | category | flops | bytes accessed | tf_op | source)
XLA Modules:
  0.0 80.3 jit_solution(2485414457002055931)
XLA Ops:
  1.3 77.5 %vti_window.1 = f32[2,8,8,256]{3,2,1,0:T(8,128)} custom-call(f32[8,8,256]{2,1,0:T(8,128)} %vel.1, f32[8,8,256]{2,1,0:T(8,128)} %eps.1, f32[1,4,8,128,256]{4,3,2,1,0:T(8,128)} %fwd.1, f32[1,4,8,128,256]{4,3,2,1,0:T(8,128)} %adj.1, s32[1]{0:T(128)S(6)} %copy.10.src, f32[1,3]{1,0:T(1,128)} %wav.1, s32[1,256]{1,0:T(1,128)} %rec.1, f32[1,4,256]{2,1,0:T(4,128)} %res.1), custom_call_target="tpu_custom_call" | custom-call | tf_op jit(solution)/shard_map/vti_window/pallas_call | solution.py:595
  78.7 1.5 %slice_bitcast_fusion = (f32[8,8,256]{2,1,0:T(8,128)}, f32[8,8,256]{2,1,0:T(8,128)}) fusion(f32[2,8,8,256]{3,2,1,0:T(8,128)} %vti_window.1), kind=kLoop, calls=%fused_computation | loop fusion | bytes 262144 | tf_op jit(solution)/shard_map/squeeze | solution.py:606

commit v3 on v2

--- a/solution.py
+++ b/solution.py
@@ -36,6 +36,7 @@
     n_pairs = depth // 2
     near = 1 if doms == 2 else 2
     groups = ((0, near), (near, n_pairs))
+    rounds = ((0, near + 1), (near + 1, n_pairs))
 
     def shot_at(z, x, c):
         return (z * 2 + x) * 2 + c
@@ -143,7 +144,7 @@
             q1, 0, c, fwd.at[0, 3, pl.ds(0, 2)], fwd.at[0, 3, pl.ds(depth - 2, 2)])
 
     def block_copy(g, owner, target, send_sem):
-        low, high = groups[g]
+        low, high = rounds[g]
         part = gath.at[owner, pl.ds(low, high - low)]
         return pltpu.make_async_remote_copy(
             src_ref=part, dst_ref=part, send_sem=send_sem, recv_sem=g_recv.at[g, owner],
@@ -195,7 +196,7 @@
                 stretch[pair, part, :] = 1.0 + 2.0 * gath[s, place, 1]
             return carry
 
-        lax.fori_loop(*groups[g], spread, 0)
+        lax.fori_loop(*rounds[g], spread, 0)
 
     for copy in own:
         copy.wait()
@@ -410,8 +411,8 @@
             pending = commit
         pending()
 
-    def sweep(body, g):
-        low, high = groups[g]
+    def sweep(body, g, span=None):
+        low, high = groups[g] if span is None else span
 
         def turn(i, carry):
             j = i // n_chunks
@@ -445,22 +446,36 @@
     near_sweep(functools.partial(forward, 0), (q1, 0), (q0, 1))
     for d in range(2, zs):
         from_z_side(1, d)
-    inject_moment(2)
-    inject_moment(1)
+    middle, rest = (near, near + 1), rounds[1]
+    sweep(start_adjoint, 1, middle)
+    sweep(functools.partial(forward, 0), 1, middle)
     for d in range(zs):
         from_x_side(1, d)
-    inject_moment(0)
+
+    def near_adjoint(turn):
+        near_sweep(functools.partial(adjoint, STEPS - 1 - turn), (S_[turn % 2], 4 + turn),
+                   (S_[(turn + 1) % 2], 5 + turn))
+
+    if doms == 2:
+        near_adjoint(0)
+    for k in reversed(range(STEPS - 1)):
+        inject_moment(k)
     finish_gather(1)
-    sweep(start_adjoint, 1)
-    sweep(functools.partial(forward, 0), 1)
+    sweep(start_adjoint, 1, rest)
+    if doms != 2:
+        near_adjoint(0)
+    sweep(functools.partial(forward, 0), 1, rest)
     for turn in range(STEPS - 1):
         k = STEPS - 1 - turn
-        near_sweep(functools.partial(adjoint, k), (S_[turn % 2], 4 + turn),
-                   (S_[(turn + 1) % 2], 5 + turn))
-        sweep(functools.partial(adjoint, k), 1)
+        if turn > 0:
+            near_adjoint(turn)
+            sweep(functools.partial(adjoint, k), 1)
         f = turn + 1
         if f + 1 < STEPS:
             near_sweep(functools.partial(forward, f), (Q_[(f + 1) % 2], f), (Q_[f % 2], f + 1))
+        if turn == 0:
+            sweep(functools.partial(adjoint, k), 1)
+        if f + 1 < STEPS:
             sweep(functools.partial(forward, f), 1)
 
     def sum_copy(g, owner, target, index, landing, send_sem, recv_sem):

time: 80.5 us -> 83 us (1.031)
  Pallas kernels: 77.5 us -> 80 us
    pallas_call x1, Pallas kernels: 77.5 us -> 80 us  [on_device(): pl.pallas_call(functools.partial(kernel, shots, doms, chunk, 16), out_sha...]
where the time goes in v3:
time: 83 us; the launch traced here: 82.8 us
  Pallas kernels  80 us (96%)
  local copies, waits for them, and re-layouts  1.53 us (2%)
  between operations  1.29 us (2%)
    pallas_call x1, Pallas kernels, on_device(): pl.pallas_call(functools.partial(kernel, shots, doms, chunk, 16), out_sha...  80 us

profile of v3, /device:TPU:0, one launch (start us, length us, event | category | flops | bytes accessed | tf_op | source)
XLA Modules:
  0.0 82.8 jit_solution(2651459788873646807)
XLA Ops:
  1.3 80.0 %vti_window.1 = f32[2,8,8,256]{3,2,1,0:T(8,128)} custom-call(f32[8,8,256]{2,1,0:T(8,128)} %vel.1, f32[8,8,256]{2,1,0:T(8,128)} %eps.1, f32[1,4,8,128,256]{4,3,2,1,0:T(8,128)} %fwd.1, f32[1,4,8,128,256]{4,3,2,1,0:T(8,128)} %adj.1, s32[1]{0:T(128)S(6)} %copy.10.src, f32[1,3]{1,0:T(1,128)} %wav.1, s32[1,256]{1,0:T(1,128)} %rec.1, f32[1,4,256]{2,1,0:T(4,128)} %res.1), custom_call_target="tpu_custom_call" | custom-call | tf_op jit(solution)/shard_map/vti_window/pallas_call | solution.py:610
  81.3 1.5 %slice_bitcast_fusion = (f32[8,8,256]{2,1,0:T(8,128)}, f32[8,8,256]{2,1,0:T(8,128)}) fusion(f32[2,8,8,256]{3,2,1,0:T(8,128)} %vti_window.1), kind=kLoop, calls=%fused_computation | loop fusion | bytes 262144 | tf_op jit(solution)/shard_map/squeeze | solution.py:621

commit v4 on v2

--- a/solution.py
+++ b/solution.py
@@ -401,10 +401,13 @@
 
         return commit
 
-    def run(body, z, r0, place=None, sub=None):
+    def row_of(r0, offset):
+        return offset if isinstance(r0, int) else pl.multiple_of(r0 + offset, block)
+
+    def run(body, z, r0, place=None, sub=None, size=chunk):
         pending = None
-        for i in range(chunk // block):
-            commit = body(z, pl.multiple_of(r0 + i * block, block), place, sub)
+        for i in range(size // block):
+            commit = body(z, row_of(r0, i * block), place, sub)
             if pending is not None:
                 pending()
             pending = commit
@@ -414,13 +417,11 @@
         low, high = groups[g]
 
         def turn(i, carry):
-            j = i // n_chunks
-            place, sub = low + j // 2, lax.rem(j, 2)
-            r0 = pl.multiple_of(lax.rem(i, n_chunks) * chunk, chunk)
-            run(body, first_layer_of(place) + sub, r0, place, sub)
+            place, sub = low + i // 2, lax.rem(i, 2)
+            run(body, first_layer_of(place) + sub, 0, place, sub, width)
             return carry
 
-        lax.fori_loop(0, (high - low) * 2 * n_chunks, turn, 0)
+        lax.fori_loop(0, (high - low) * 2, turn, 0)
 
     def near_sweep(body, waits=None, sends=None):
         def stripe(c, carry):

time: 80.5 us -> 79.3 us (0.985)
  Pallas kernels: 77.5 us -> 76.3 us
    pallas_call x1, Pallas kernels: 77.5 us -> 76.3 us  [on_device(): pl.pallas_call(functools.partial(kernel, shots, doms, chunk, 16), out_sha...]
where the time goes in v4:
time: 79.3 us; the launch traced here: 79.1 us
  Pallas kernels  76.3 us (96%)
  local copies, waits for them, and re-layouts  1.53 us (2%)
  between operations  1.29 us (2%)
    pallas_call x1, Pallas kernels, on_device(): pl.pallas_call(functools.partial(kernel, shots, doms, chunk, 16), out_sha...  76.3 us

profile of v4, /device:TPU:0, one launch (start us, length us, event | category | flops | bytes accessed | tf_op | source)
XLA Modules:
  0.0 79.1 jit_solution(3706776732815018893)
XLA Ops:
  1.3 76.3 %vti_window.1 = f32[2,8,8,256]{3,2,1,0:T(8,128)} custom-call(f32[8,8,256]{2,1,0:T(8,128)} %vel.1, f32[8,8,256]{2,1,0:T(8,128)} %eps.1, f32[1,4,8,128,256]{4,3,2,1,0:T(8,128)} %fwd.1, f32[1,4,8,128,256]{4,3,2,1,0:T(8,128)} %adj.1, s32[1]{0:T(128)S(6)} %copy.10.src, f32[1,3]{1,0:T(1,128)} %wav.1, s32[1,256]{1,0:T(1,128)} %rec.1, f32[1,4,256]{2,1,0:T(4,128)} %res.1), custom_call_target="tpu_custom_call" | custom-call | tf_op jit(solution)/shard_map/vti_window/pallas_call | solution.py:596
  77.6 1.5 %slice_bitcast_fusion = (f32[8,8,256]{2,1,0:T(8,128)}, f32[8,8,256]{2,1,0:T(8,128)}) fusion(f32[2,8,8,256]{3,2,1,0:T(8,128)} %vti_window.1), kind=kLoop, calls=%fused_computation | loop fusion | bytes 262144 | tf_op jit(solution)/shard_map/squeeze | solution.py:607
